TPU v7x, 32 devices: a whole 2x2x4 slice. The times are simulated.
32 devices in a mesh: groups: 2 (over x), pts: 8 (over z, y), sub: 2 (over core).
Axes of the slice: x: 2, y: 2, z: 4, core: 2. Of those that a mesh axis runs over, the one named last changes fastest.
Arguments:
- points: float32 [8192, 64], P(('groups', 'pts', 'sub')), parts along dimension 0, may hold values from -6 to 6
- inverse_scale: float32 [64], replicated, may hold values from 0.03 to 0.15
- noise_level: float32 [8192], P(('groups', 'pts', 'sub')), parts along dimension 0, may hold values from 0.3 to 3
- probes: float32 [8192, 32], P(('groups', 'pts', 'sub')), parts along dimension 0, may hold values from -6 to 6
- task_cov: float32 [8, 8], replicated, may hold values from 0 to 1.5, as said below
Outputs:
- solution: float32 [8192, 32], P(('groups', 'pts', 'sub')), parts along dimension 0
- residual: float32 [8192, 32], P(('groups', 'pts', 'sub')), parts along dimension 0
There are 2 independent parts, one for each index of `groups`. A program takes and returns all parts, laid end to end along the dimension named above; an argument that names none is the same for every part. Nothing has to cross between parts.
Inputs may be any that keep to these rules, and one draw needn't show every extreme that they name: task_cov is symmetric with positive entries, and each diagonal entry exceeds the sum of the other entries of its row.
All inputs are finite; a program needn't handle non-finite values.
Results may differ from a plain program's by a relative error of at most 0.0003.
Values sent between devices are 32-bit elements; how exact they have to be, the bound alone decides.
A program may use at most 64 MiB of HBM per device.

v0:
```python
import jax
import jax.numpy as jnp
from jax import lax
from jax.sharding import PartitionSpec as P

ITERS = 3


SQRT_FIVE = 5.0**0.5
HIGHEST = lax.Precision.HIGHEST


def matern(rows_scaled, rows_square, cols_scaled, cols_square):
    inner = lax.dot_general(
        rows_scaled,
        cols_scaled,
        (((1,), (1,)), ((), ())),
        precision=HIGHEST,
        preferred_element_type=jnp.float32,
    )
    squared = jnp.maximum(rows_square[:, None] + cols_square[None, :] - 2.0 * inner, 0.0)
    distance = jnp.sqrt(squared)
    return (1.0 + SQRT_FIVE * distance + 5.0 / 3.0 * squared) * jnp.exp(-SQRT_FIVE * distance)


def squares(residual):
    return lax.psum(jnp.sum(residual * residual, axis=0), ("pts", "sub"))


def local(points, inverse_scale, noise_level, probes, task_cov):
    row_count = points.shape[0]
    block_count = lax.axis_size("pts")
    half_count = lax.axis_size("sub")
    my_block = lax.axis_index("pts")
    my_half = lax.axis_index("sub")
    scaled = points * inverse_scale[None, :]
    square = jnp.sum(scaled * scaled, axis=1)
    rounds = block_count - 1
    round_ids = jnp.arange(rounds)
    opposite = jnp.mod(2 * round_ids - my_block, rounds)
    partners = jnp.where(
        my_block == rounds, round_ids, jnp.where(opposite == my_block, rounds, opposite)
    )
    weight_row = lax.dynamic_slice_in_dim(task_cov, my_block, 1, 0)[0]
    block_width = half_count * row_count
    all_scaled, all_square = (
        lax.all_gather(scaled, ("pts", "sub"), axis=0, tiled=True),
        lax.all_gather(square, ("pts", "sub"), axis=0, tiled=True),
    )
    solution = jnp.zeros_like(probes)
    residual = probes
    direction = probes
    norm_now = squares(residual)
    for iteration in range(ITERS):
        vector = direction
        all_vector = lax.all_gather(vector, ("pts", "sub"), axis=0, tiled=True)
        own_start = my_block * block_width
        tile = (
            matern(
                scaled,
                square,
                lax.dynamic_slice_in_dim(all_scaled, own_start, block_width, 0),
                lax.dynamic_slice_in_dim(all_square, own_start, block_width, 0),
            )
            * weight_row[my_block]
        )
        image = jnp.dot(
            tile,
            lax.dynamic_slice_in_dim(all_vector, own_start, block_width, 0),
            precision=HIGHEST,
            preferred_element_type=jnp.float32,
        )

        def one_round(index, carry):
            image_sum, returned = carry
            partner = partners[index]
            half = jnp.where(my_block < partner, my_half, 1 - my_half)
            start = (partner * half_count + half) * row_count
            part_tile = (
                matern(
                    scaled,
                    square,
                    lax.dynamic_slice_in_dim(all_scaled, start, row_count, 0),
                    lax.dynamic_slice_in_dim(all_square, start, row_count, 0),
                )
                * weight_row[partner]
            )
            image_sum = image_sum + jnp.dot(
                part_tile,
                lax.dynamic_slice_in_dim(all_vector, start, row_count, 0),
                precision=HIGHEST,
                preferred_element_type=jnp.float32,
            )
            mirror_term = lax.dot_general(
                part_tile,
                vector,
                (((0,), (0,)), ((), ())),
                precision=HIGHEST,
                preferred_element_type=jnp.float32,
            )
            returned = lax.dynamic_update_slice_in_dim(returned, mirror_term, start, 0)
            return (image_sum, returned)

        image, returned = lax.fori_loop(0, rounds, one_round, (image, jnp.zeros_like(all_vector)))
        image = image + lax.psum_scatter(returned, ("pts", "sub"), scatter_dimension=0, tiled=True)
        image = image + noise_level[:, None] * vector
        alpha = norm_now / lax.psum(jnp.sum(direction * image, axis=0), ("pts", "sub"))
        solution = solution + alpha[None, :] * direction
        residual = residual - alpha[None, :] * image
        norm_next = squares(residual)
        direction = residual + (norm_next / norm_now)[None, :] * direction
        norm_now = norm_next
    return (solution, residual)


def solution(mesh):
    return jax.shard_map(
        local,
        mesh=mesh,
        in_specs=(
            P(("groups", "pts", "sub"), None),
            P(),
            P(("groups", "pts", "sub")),
            P(("groups", "pts", "sub"), None),
            P(),
        ),
        out_specs=(P(("groups", "pts", "sub"), None), P(("groups", "pts", "sub"), None)),
        check_vma=False,
    )
```

profile of v0, /device:TPU:0, one launch (start us, length us, event | category | flops | bytes accessed | tf_op | source)
XLA Modules:
  0.0 588.2 jit_solution(259419775999124391)
XLA Ops:
  10.4 23.1 %all-gather = f32[16,1,256]{2,1,0:T(1,128)S(1)} all-gather(f32[1,1,256]{2,1,0:T(1,128)S(1)} %bitcast.95), channel_id=1, replica_groups=mesh['groups'=2,'pts'=8,'sub'=2] {'pts','sub'}, dimensions={0}, use_global_device_ids=true | all-gather | bytes 17408 | tf_op jit(solution)/shard_map/all_gather | solution.py:48
  35.7 36.0 %all_gather.17 = f32[4096,32]{1,0:T(8,128)S(1)} all-gather(f32[256,32]{1,0:T(8,128)S(1)} %copy.14), channel_id=1, replica_groups=mesh['groups'=2,'pts'=8,'sub'=2] {'pts','sub'}, dimensions={0}, use_global_device_ids=true | all-gather | bytes 557056 | tf_op jit(solution)/shard_map/all_gather | solution.py:56
  71.7 2.5 multiply_multiply_fusion.3
  74.9 50.2 %while.48 = (s32[]{:T(128)}, f32[256,32]{0,1:T(8,128)S(1)}, f32[4096,32]{0,1:T(8,128)S(1)}, f32[256]{0:T(256)S(1)}, s32[7]{0:T(128)S(1)}, /*index=5*/s32[]{:T(12...) while((s32[]{:T(128)}, f32[256,32]{0,1:T(8,128)S(1)}, ...), condition=%wide.region_4.5_spmd, body=%wide.region_3.4_spmd.sunk | while | flops 101392400 | bytes 1250139 | solution.py:104
  79.3 2.0 multiply_multiply_fusion.7
  100.8 2.0 multiply_multiply_fusion.7
  108.0 2.0 multiply_multiply_fusion.7
  122.3 2.0 multiply_multiply_fusion.7
  126.0 53.2 %reduce-scatter.4.cloned.1.call-done = f32[256,32]{0,1:T(8,128)} async-done(((f32[4096,32]{0,1:T(8,128)}), f32[256,32]{0,1:T(8,128)}) %reduce-scatter.4.cloned.1.call-update) | async-done | bytes 32784 | tf_op jit(solution)/shard_map/reduce_scatter | solution.py:105
  180.0 29.6 %all-reduce = (f32[32]{0:T(128)S(1)}, f32[32]{0:T(128)S(1)}) all-reduce(f32[32]{0:T(128)S(1)} %get-tuple-element.881, f32[32]{0:T(128)S(1)} %get-tuple-element.880), channel_id=1, replica_groups=mesh['groups'=2,'pts'=8,'sub'=2] {'pts','sub'}, use_global_device_ids=true, to_apply=%region_1.2 | all-reduce | flops 64 | bytes 512 | tf_op jit(solution)/shard_map/psum | solution.py:27
  210.6 29.5 %psum.44 = f32[32]{0:T(128)S(1)} all-reduce(f32[32]{0:T(128)S(1)} %get-tuple-element.970), channel_id=1, replica_groups=mesh['groups'=2,'pts'=8,'sub'=2] {'pts','sub'}, use_global_device_ids=true, to_apply=%region_9.10 | all-reduce | flops 32 | bytes 256 | tf_op jit(solution)/shard_map/psum | solution.py:27
  240.2 18.7 %all_gather.18 = f32[4096,32]{0,1:T(8,128)S(1)} all-gather(f32[256,32]{0,1:T(8,128)S(1)} %multiply_add_fusion.4), channel_id=1, replica_groups=mesh['groups'=2,'pts'=8,'sub'=2] {'pts','sub'}, dimensions={0}, use_global_device_ids=true | all-gather | bytes 557056 | tf_op jit(solution)/shard_map/all_gather | solution.py:56
  259.6 49.6 %while.49 = (s32[]{:T(128)}, f32[256,32]{0,1:T(8,128)S(1)}, f32[4096,32]{0,1:T(8,128)S(1)}, f32[256]{0:T(256)S(1)}, s32[7]{0:T(128)S(1)}, /*index=5*/s32[]{:T(12...) while((s32[]{:T(128)}, f32[256,32]{0,1:T(8,128)S(1)}, ...), condition=%wide.region_11.12_spmd, body=%wide.region_10.11_spmd.sunk | while | flops 101392400 | bytes 1250139 | solution.py:104
  299.4 2.0 multiply_multiply_fusion.8
  310.1 54.3 %reduce-scatter.6.cloned.1.call-done = f32[256,32]{0,1:T(8,128)} async-done(((f32[4096,32]{0,1:T(8,128)}), f32[256,32]{0,1:T(8,128)}) %reduce-scatter.6.cloned.1.call-update) | async-done | bytes 32784 | tf_op jit(solution)/shard_map/reduce_scatter | solution.py:105
  365.3 29.6 %psum.45 = f32[32]{0:T(128)S(1)} all-reduce(f32[32]{0:T(128)S(1)} %multiply_reduce_fusion.3), channel_id=1, replica_groups=mesh['groups'=2,'pts'=8,'sub'=2] {'pts','sub'}, use_global_device_ids=true, to_apply=%region_14.15 | all-reduce | flops 32 | bytes 256 | tf_op jit(solution)/shard_map/psum | solution.py:107
  395.8 29.5 %psum.46 = f32[32]{0:T(128)S(1)} all-reduce(f32[32]{0:T(128)S(1)} %get-tuple-element.968), channel_id=1, replica_groups=mesh['groups'=2,'pts'=8,'sub'=2] {'pts','sub'}, use_global_device_ids=true, to_apply=%region_16.17 | all-reduce | flops 32 | bytes 256 | tf_op jit(solution)/shard_map/psum | solution.py:27
  425.4 18.7 %all_gather.19 = f32[4096,32]{0,1:T(8,128)S(1)} all-gather(f32[256,32]{0,1:T(8,128)S(1)} %multiply_add_fusion.2), channel_id=1, replica_groups=mesh['groups'=2,'pts'=8,'sub'=2] {'pts','sub'}, dimensions={0}, use_global_device_ids=true | all-gather | bytes 557056 | tf_op jit(solution)/shard_map/all_gather | solution.py:56
  444.8 49.6 %while.50 = (s32[]{:T(128)}, f32[256,32]{0,1:T(8,128)S(1)}, f32[4096,32]{0,1:T(8,128)S(1)}, f32[256]{0:T(256)S(1)}, s32[7]{0:T(128)S(1)}, /*index=5*/s32[]{:T(12...) while((s32[]{:T(128)}, f32[256,32]{0,1:T(8,128)S(1)}, ...), condition=%wide.region_18.19_spmd, body=%wide.region_17.18_spmd.sunk | while | flops 101392400 | bytes 1250139 | solution.py:104
  449.2 2.0 multiply_multiply_fusion.9
  463.4 2.0 multiply_multiply_fusion.9
  484.7 2.0 multiply_multiply_fusion.9
  495.3 54.4 %reduce-scatter.8.cloned.1.call-done = f32[256,32]{0,1:T(8,128)} async-done(((f32[4096,32]{0,1:T(8,128)}), f32[256,32]{0,1:T(8,128)}) %reduce-scatter.8.cloned.1.call-update) | async-done | bytes 32784 | tf_op jit(solution)/shard_map/reduce_scatter | solution.py:105
  550.5 29.7 %psum.47 = f32[32]{0:T(128)S(1)} all-reduce(f32[32]{0:T(128)S(1)} %multiply_reduce_fusion.1), channel_id=1, replica_groups=mesh['groups'=2,'pts'=8,'sub'=2] {'pts','sub'}, use_global_device_ids=true, to_apply=%region_21.22 | all-reduce | flops 32 | bytes 256 | tf_op jit(solution)/shard_map/psum | solution.py:107
  (167 shorter events, 83.2 us)
Async XLA Ops:
  7.2 64.5 %all-gather.3.cloned.1.call-start = ((), (), s32[]{:S(2)}) async-start(), calls=%async_computation.3 | async-start | bytes 2228224 | tf_op jit(solution)/shard_map/all_gather | solution.py:47
  9.5 62.2 %copy-start.4 = (f32[256,64]{1,0:T(8,128)S(1)}, f32[256,64]{1,0:T(8,128)}, u32[]{:S(2)}) copy-start(f32[256,64]{1,0:T(8,128)} %get-tuple-element.1361) | copy-start | bytes 196612
  9.5 169.7 %reduce-scatter.4.cloned.1.call-start = ((), (), s32[]{:S(2)}) async-start(), calls=%async_computation.4 | async-start | bytes 557056 | tf_op jit(solution)/shard_map/reduce_scatter | solution.py:105
  35.6 39.2 %copy-start = (f32[256,32]{0,1:T(8,128)S(1)}, f32[256,32]{0,1:T(8,128)}, u32[]{:S(2)}) copy-start(f32[256,32]{0,1:T(8,128)} %param.14) | copy-start | bytes 98308
  74.9 104.3 %copy-start.5 = (f32[256]{0:T(256)S(1)}, f32[256]{0:T(256)}, u32[]{:S(2)}) copy-start(f32[256]{0:T(256)} %param.13) | copy-start | bytes 3076
  125.1 0.8 copy-start.2
  125.9 238.5 %reduce-scatter.6.cloned.1.call-start = ((), (), s32[]{:S(2)}) async-start(), calls=%async_computation.5 | async-start | bytes 557056 | tf_op jit(solution)/shard_map/reduce_scatter | solution.py:105
  309.2 0.8 copy-start.3
  310.1 239.6 %reduce-scatter.8.cloned.1.call-start = ((), (), s32[]{:S(2)}) async-start(), calls=%async_computation.6 | async-start | bytes 557056 | tf_op jit(solution)/shard_map/reduce_scatter | solution.py:105
  494.5 0.8 copy-start.1
Sparse Core Ops, SparseCore 0:
  10.2 53.1 all-gather.2
  126.0 53.0 reduce-scatter.3
  310.2 54.1 reduce-scatter.5
  495.4 54.2 reduce-scatter.7
where the time goes:
time: 591 us; the launch traced here: 588 us
  blocking collectives  244 us (41%)
  waiting for transfers between devices  162 us (27%)
  loops' own time  66 us (11%)
  matrix products  61.1 us (10%)
  local copies, waits for them, and re-layouts  33.2 us (6%)
  between operations  13.9 us (2%)
  other arithmetic  7.52 us (1%)
    reduce_scatter x3, waiting for transfers between devices, local(): lax.psum_scatter(returned, ('pts', 'sub'), scatter_dimension=0, tiled=True)  162 us
    psum x3, blocking collectives, squares(): return lax.psum(jnp.sum(residual * residual, axis=0), ('pts', 'sub'))  88.6 us
    all_gather x3, blocking collectives, local(): all_vector = lax.all_gather(vector, ('pts', 'sub'), axis=0, tiled=True)  73.4 us
    another operation x3, loops' own time, local(): lax.fori_loop(0, rounds, one_round, (image, jnp.zeros_like(all_vector)))  66 us
    psum x2, blocking collectives, local(): lax.psum(jnp.sum(direction * image, axis=0), ('pts', 'sub'))  59.2 us
    dot_general x22, matrix products, matern(): lax.dot_general(rows_scaled, cols_scaled, (((1,), (1,)), ((), ())), preci...  45.4 us
    all_gather x1, blocking collectives, local(): lax.all_gather(square, ('pts', 'sub'), axis=0, tiled=True)  23.1 us
    dynamic_slice x21, local copies, waits for them, and re-layouts, one_round(): weight_row[partner]  12.5 us
  transfers between devices with their start and end apart: 4, of which 3 were waited for; matrix products, arithmetic and copies ran while one was open for 1% of the time, Pallas kernels for 0%

commit v1 on v0

v1 whole, which is shorter than its diff:
```python
import functools

import jax
import jax.numpy as jnp
from jax import lax
from jax.experimental import pallas as pl
from jax.experimental.pallas import tpu as pltpu
from jax.sharding import PartitionSpec as P

ITERS = 3
PAIR = 2
MESH = pl.DeviceIdType.MESH
SQRT_FIVE = 5.0**0.5
F32, BF16 = jnp.float32, jnp.bfloat16


def halves(x):
    hi = x.astype(BF16)
    return hi, (x - hi.astype(F32)).astype(BF16)


def augmented(scaled):
    features, width = scaled.shape
    hi, lo = (part.astype(F32) for part in halves(scaled))
    square = jnp.sum(hi * hi + 2.0 * (hi * lo), axis=0, keepdims=True)
    top, rest = (part.astype(F32) for part in halves(square))
    mid = rest
    low = square - top - mid
    pad = (-3 * features) % 128
    row = lax.broadcasted_iota(jnp.int32, (pad, width), 0)
    three = jnp.where(row % 3 == 0, top, jnp.where(row % 3 == 1, mid, low))
    one = jnp.ones_like(three)
    zero = jnp.zeros_like(three)
    left = jnp.where(row < 3, three, jnp.where(row < 6, one, zero))
    right = jnp.where(row < 3, one, jnp.where(row < 6, three, zero))
    return (
        jnp.concatenate([-2.0 * hi, -2.0 * hi, -2.0 * lo, left], axis=0),
        jnp.concatenate([hi, lo, hi, right], axis=0),
    )


def kernel(
    nz, ny, ns, points_ref, inverse_ref, noise_ref, probes_ref, weights_ref, sol_ref, res_ref,
    col_pts, row_pts, vec, part_out, part, rr_buf, dot_buf, k_hi, k_lo, right_fac, sq_dist,
    pts_z_send, pts_z_recv, pts_q_send, pts_q_recv, vec_send, vec_recv,
    part_send, part_recv, rr_send, rr_recv, dot_send, dot_recv,
):
    n, m = probes_ref.shape
    nq = ny * ns
    block = lax.axis_index("pts")
    core = lax.axis_index("sub")
    z, y = block // ny, block % ny

    def device(dz, a, b):
        return {"pts": ((z + dz) % nz) * ny + (y + a) % ny, "sub": (core + b) % ns}

    q_offsets = [(a, b) for a in range(ny) for b in range(ns)]
    offsets = [(dz, a, b) for dz in range(nz) for a, b in q_offsets]

    def mirror_q(j):
        a, b = q_offsets[j]
        return ((-a) % ny) * ns + (-b) % ns

    def mirror(i):
        dz, a, b = offsets[i]
        return ((-dz) % nz) * nq + mirror_q(a * ns + b)

    sends = []

    def send(src, dst, send_sem, recv_sem, target):
        copy = pltpu.make_async_remote_copy(
            src_ref=src, dst_ref=dst, send_sem=send_sem, recv_sem=recv_sem,
            device_id=target, device_id_type=MESH,
        )
        copy.start()
        sends.append(copy)

    def arrived(dst, send_sem, recv_sem):
        pltpu.make_async_remote_copy(
            src_ref=dst, dst_ref=dst, send_sem=send_sem, recv_sem=recv_sem,
            device_id=device(1, 0, 0), device_id_type=MESH,
        ).wait_recv()

    barrier = pltpu.get_barrier_semaphore()
    for i in range(1, nz * nq):
        pl.semaphore_signal(barrier, inc=1, device_id=device(*offsets[i]), device_id_type=MESH)

    scaled = (points_ref[...] * (inverse_ref[...] * SQRT_FIVE)).T
    col_pts[0] = scaled
    own_probes = probes_ref[...].T
    vec[0, 0] = own_probes

    pl.semaphore_wait(barrier, nz * nq - 1)

    for dz in range(1, nz):
        k = nz - dz
        send(col_pts.at[0], col_pts.at[k], pts_z_send.at[k], pts_z_recv.at[k], device(dz, 0, 0))
    for j in range(1, nq):
        k = mirror_q(j)
        send(col_pts.at[0], row_pts.at[k], pts_q_send.at[k], pts_q_recv.at[k], device(0, *q_offsets[j]))

    def gather_vector(t):
        for dz in range(1, nz):
            k = nz - dz
            send(vec.at[t, 0], vec.at[t, k], vec_send.at[t, k], vec_recv.at[t, k], device(dz, 0, 0))

    def vector_block(t, k):
        if k:
            arrived(vec.at[t, k], vec_send.at[t, k], vec_recv.at[t, k])
        return vec[t, k]

    gather_vector(0)

    for j in range(nq):
        if j:
            arrived(row_pts.at[j], pts_q_send.at[j], pts_q_recv.at[j])
            factor = augmented(row_pts[j])[1]
        else:
            factor = augmented(scaled)[1]
        right_fac[:, j * n:(j + 1) * n] = factor.astype(BF16)

    half = ns * n
    for k in range(nz):
        if k:
            arrived(col_pts.at[k], pts_z_send.at[k], pts_z_recv.at[k])
        left = augmented(col_pts[k])[0].T.astype(BF16)
        sq_dist[...] = jnp.dot(left, right_fac[...], preferred_element_type=F32)
        column_block = ((z + k) % nz) * ny + y
        weight = [weights_ref[z * ny + (y + a) % ny, column_block] for a in range(ny)]

        def rows(i, carry):
            at = pl.multiple_of(i * 16, 16)
            for a in range(ny):
                span = slice(a * half, (a + 1) * half)
                sq = jnp.maximum(sq_dist[pl.ds(at, 16), span], 1e-30)
                dist = sq * lax.rsqrt(sq)
                value = ((1.0 + dist + sq * (1.0 / 3.0)) * weight[a]) * jnp.exp(-dist)
                hi, lo = halves(value)
                k_hi[pl.ds(k * n + at, 16), span] = hi
                k_lo[pl.ds(k * n + at, 16), span] = lo
            return carry

        lax.fori_loop(0, n // 16, rows, 0)

    eye = lax.broadcasted_iota(jnp.int32, (m, 128), 0) == lax.broadcasted_iota(jnp.int32, (m, 128), 1)

    def to_row(column):
        return jnp.sum(jnp.where(eye, column, 0.0), axis=0, keepdims=True)

    def to_column(row):
        return jnp.sum(jnp.where(eye, row, 0.0), axis=1, keepdims=True)

    noise = noise_ref[...]
    residual = [vector_block(0, k) for k in range(nz)]
    direction = image = norm_now = None
    answer = jnp.zeros_like(own_probes)
    for t in range(ITERS):
        norm_part = sum(jnp.sum(r * r, axis=1, keepdims=True) for r in residual)
        rr_buf[t, 0] = to_row(norm_part)
        for j in range(1, nq):
            s = mirror_q(j)
            send(rr_buf.at[t, 0], rr_buf.at[t, s], rr_send.at[t, s], rr_recv.at[t, s], device(0, *q_offsets[j]))
        pieces = [halves(r) for r in residual]
        hi = jnp.concatenate([p[0] for p in pieces], axis=1)
        lo = jnp.concatenate([p[1] for p in pieces], axis=1)
        both = jnp.concatenate([hi, lo], axis=0)

        def partial(j):
            span = slice(j * n, (j + 1) * n)
            two = jnp.dot(both, k_hi[:, span], preferred_element_type=F32)
            return two[:m] + two[m:] + jnp.dot(hi, k_lo[:, span], preferred_element_type=F32)

        for j in reversed(range(1, nq)):
            part_out[t, j] = partial(j)
            s = mirror_q(j)
            send(part_out.at[t, j], part.at[t, s], part_send.at[t, s], part_recv.at[t, s], device(0, *q_offsets[j]))
        fresh = partial(0) + noise * residual[0]
        norm_row = rr_buf[t, 0]
        for j in range(1, nq):
            arrived(rr_buf.at[t, j], rr_send.at[t, j], rr_recv.at[t, j])
            norm_row = norm_row + rr_buf[t, j]
        norm_next = to_column(norm_row)
        for j in range(1, nq):
            arrived(part.at[t, j], part_send.at[t, j], part_recv.at[t, j])
            fresh = fresh + part[t, j]
        if t == 0:
            image, direction = fresh, residual
        else:
            beta = norm_next / norm_now
            image = fresh + beta * image
            direction = [r + beta * d for r, d in zip(residual, direction)]
        norm_now = norm_next
        if t + 1 < ITERS:
            vec[t + 1, 0] = image
            gather_vector(t + 1)
        dot_buf[t, 0] = to_row(jnp.sum(direction[0] * image, axis=1, keepdims=True))
        for i in range(1, nz * nq):
            s = mirror(i)
            send(dot_buf.at[t, 0], dot_buf.at[t, s], dot_send.at[t, s], dot_recv.at[t, s], device(*offsets[i]))
        dot_row = dot_buf[t, 0]
        for i in range(1, nz * nq):
            arrived(dot_buf.at[t, i], dot_send.at[t, i], dot_recv.at[t, i])
            dot_row = dot_row + dot_buf[t, i]
        alpha = norm_now / to_column(dot_row)
        answer = answer + alpha * direction[0]
        if t + 1 < ITERS:
            residual = [residual[0] - alpha * image] + [
                residual[k] - alpha * vector_block(t + 1, k) for k in range(1, nz)
            ]
        else:
            residual = [residual[0] - alpha * image]
    sol_ref[...] = answer.T
    res_ref[...] = residual[0].T
    for copy in sends:
        copy.wait_send()


def solution(mesh):
    ny = PAIR
    nz, ns = mesh.shape["pts"] // ny, mesh.shape["sub"]
    nq = ny * ns

    def local(points, inverse_scale, noise_level, probes, task_cov):
        n, features = points.shape
        m = probes.shape[1]
        depth = 3 * features + (-3 * features) % 128
        vmem = pl.BlockSpec(memory_space=pltpu.VMEM)
        dma = pltpu.SemaphoreType.DMA
        out = jax.ShapeDtypeStruct((n, m), F32)
        return pl.pallas_call(
            functools.partial(kernel, nz, ny, ns),
            out_shape=(out, out),
            in_specs=[vmem] * 4 + [pl.BlockSpec(memory_space=pltpu.SMEM)],
            out_specs=(vmem, vmem),
            scratch_shapes=[
                pltpu.VMEM((nz, features, n), F32),
                pltpu.VMEM((nq, features, n), F32),
                pltpu.VMEM((ITERS, nz, m, n), F32),
                pltpu.VMEM((ITERS, nq, m, n), F32),
                pltpu.VMEM((ITERS, nq, m, n), F32),
                pltpu.VMEM((ITERS, nq, 1, 128), F32),
                pltpu.VMEM((ITERS, nz * nq, 1, 128), F32),
                pltpu.VMEM((nz * n, nq * n), BF16),
                pltpu.VMEM((nz * n, nq * n), BF16),
                pltpu.VMEM((depth, nq * n), BF16),
                pltpu.VMEM((n, nq * n), F32),
                dma((nz,)), dma((nz,)), dma((nq,)), dma((nq,)),
                dma((ITERS, nz)), dma((ITERS, nz)),
                dma((ITERS, nq)), dma((ITERS, nq)),
                dma((ITERS, nq)), dma((ITERS, nq)),
                dma((ITERS, nz * nq)), dma((ITERS, nz * nq)),
            ],
            compiler_params=pltpu.CompilerParams(
                collective_id=0, has_side_effects=True, vmem_limit_bytes=48 * 2**20
            ),
        )(points, inverse_scale[None, :], noise_level[None, :], probes, task_cov)

    rows = P(("groups", "pts", "sub"), None)
    return jax.shard_map(
        local,
        mesh=mesh,
        in_specs=(rows, P(), P(("groups", "pts", "sub")), rows, P()),
        out_specs=(rows, rows),
        check_vma=False,
    )
```

time: 591 us -> 50.1 us (0.08)
  blocking collectives: 244 us -> 0 us
  waiting for transfers between devices: 162 us -> 0 us
  loops' own time: 66 us -> 0 us
  matrix products: 61.1 us -> 0 us
  Pallas kernels: 0 us -> 46.2 us
  local copies, waits for them, and re-layouts: 33.2 us -> 3 us
  between operations: 13.9 us -> 0.68 us
  other arithmetic: 7.52 us -> 0 us
    reduce_scatter x3 -> x0, waiting for transfers between devices: 162 us -> none  [local(): lax.psum_scatter(returned, ('pts', 'sub'), scatter_dimension=0, tiled=True)]
    psum x5 -> x0, blocking collectives: 148 us -> none  [the longest x3 88.6 us: squares(): return lax.psum(jnp.sum(residual * residual, axis=0), ('pts', 'sub'))]
    all_gather x4 -> x0, blocking collectives: 96.5 us -> none  [the longest x3 73.4 us: local(): all_vector = lax.all_gather(vector, ('pts', 'sub'), axis=0, tiled=True)]
    another operation x3 -> x0, loops' own time: 66 us -> none  [local(): lax.fori_loop(0, rounds, one_round, (image, jnp.zeros_like(all_vector)))]
    dot_general x67 -> x0, matrix products: 61.1 us -> none  [the longest x22 45.4 us: matern(): lax.dot_general(rows_scaled, cols_scaled, (((1,), (1,)), ((), ())), preci...]
    pallas_call x0 -> x1, Pallas kernels: none -> 46.2 us  [local(): pl.pallas_call(functools.partial(kernel, nz, ny, ns), out_shape=(out, out...]
    dynamic_slice x65 -> x0, local copies, waits for them, and re-layouts: 28 us -> none  [the longest x21 12.5 us: one_round(): weight_row[partner]]
  transfers between devices with their start and end apart: 4 -> 0, of which waited for: 3 -> 0; matrix products, arithmetic and copies ran while one was open for 1% -> 0% of each run, Pallas kernels for 0% -> 0%
where the time goes in v1:
time: 50.1 us; the launch traced here: 49.9 us
  Pallas kernels  46.2 us (92%)
  local copies, waits for them, and re-layouts  3 us (6%)
  between operations  0.68 us (1%)
    pallas_call x1, Pallas kernels, local(): pl.pallas_call(functools.partial(kernel, nz, ny, ns), out_shape=(out, out...  46.2 us
    unnamed x10, local copies, waits for them, and re-layouts  1.62 us
    pallas_call x2, local copies, waits for them, and re-layouts, local(): pl.pallas_call(functools.partial(kernel, nz, ny, ns), out_shape=(out, out...  1.38 us

profile of v1, /device:TPU:0, one launch (start us, length us, event | category | flops | bytes accessed | tf_op | source)
XLA Modules:
  0.0 49.9 jit_solution(2654223533308930810)
XLA Ops:
  0.6 0.0 copy-start.3
  0.6 0.9 %copy.7.points_ref = f32[256,64]{1,0:T(8,128)S(1)} copy(f32[256,64]{0,1:T(8,128)} %param.5) | data formatting | bytes 131072 | tf_op args[0]
  1.6 0.0 copy-done.3
  1.6 0.0 copy-start
  1.6 0.0 copy-start.1
  1.6 0.0 copy-start.2
  1.6 0.1 copy.8.probes_ref
  1.7 0.6 %copy-done = f32[8,8]{1,0:T(8,128)S(1)} copy-done((f32[8,8]{1,0:T(8,128)S(1)}, f32[8,8]{1,0:T(8,128)}, u32[]{:S(2)}) %copy-start) | copy-done | bytes 280
  2.3 0.0 copy-done.1
  2.3 0.0 copy-done.2
  2.3 46.2 %shard_map.68 = (f32[256,32]{1,0:T(8,128)S(1)}, f32[256,32]{1,0:T(8,128)S(1)}) custom-call(f32[256,64]{1,0:T(8,128)S(1)} %copy.7.points_ref, f32[1,64]{1,0:T(1,128)S(1)} %bitcast.3, f32[1,256]{1,0:T(1,128)S(1)} %bitcast.2, f32[256,32]{1,0:T(8,128)S(1)} %copy.8.probes_ref, f32[8,8]{1,0:T(8,128)S(1)} %copy-done), custom_call_target="tpu_custom_call" | custom-call | tf_op jit(solution)/shard_map/pallas_call | solution.py:230
  48.5 0.7 %copy.9 = f32[256,32]{0,1:T(8,128)} copy(f32[256,32]{1,0:T(8,128)S(1)} %get-tuple-element.2) | data formatting | bytes 65536 | tf_op jit(solution)/shard_map/pallas_call | solution.py:230
  49.2 0.7 %copy.10 = f32[256,32]{0,1:T(8,128)} copy(f32[256,32]{1,0:T(8,128)S(1)} %get-tuple-element.3) | data formatting | bytes 65536 | tf_op jit(solution)/shard_map/pallas_call | solution.py:230
Async XLA Ops:
  0.6 1.0 %copy-start.3 = (f32[256,32]{0,1:T(8,128)S(1)}, f32[256,32]{0,1:T(8,128)}, u32[]{:S(2)}) copy-start(f32[256,32]{0,1:T(8,128)} %param.8) | copy-start | bytes 98308
  1.6 0.7 %copy-start = (f32[8,8]{1,0:T(8,128)S(1)}, f32[8,8]{1,0:T(8,128)}, u32[]{:S(2)}) copy-start(f32[8,8]{1,0:T(8,128)} %weights_ref.1) | copy-start | bytes 772
  1.6 0.7 %copy-start.1 = (f32[256]{0:T(256)S(1)}, f32[256]{0:T(256)}, u32[]{:S(2)}) copy-start(f32[256]{0:T(256)} %param.7) | copy-start | bytes 3076
  1.6 0.7 %copy-start.2 = (f32[64]{0:T(128)S(1)}, f32[64]{0:T(128)}, u32[]{:S(2)}) copy-start(f32[64]{0:T(128)} %param.6) | copy-start | bytes 772

commit v2 on v1

--- a/solution.py
+++ b/solution.py
@@ -40,12 +40,13 @@
 
 
 def kernel(
-    nz, ny, ns, points_ref, inverse_ref, noise_ref, probes_ref, weights_ref, sol_ref, res_ref,
-    col_pts, row_pts, vec, part_out, part, rr_buf, dot_buf, k_hi, k_lo, right_fac, sq_dist,
-    pts_z_send, pts_z_recv, pts_q_send, pts_q_recv, vec_send, vec_recv,
-    part_send, part_recv, rr_send, rr_recv, dot_send, dot_recv,
+    nz, ny, ns, points_any, inverse_any, noise_any, probes_any, weights_any, sol_ref, res_ref,
+    points_ref, inverse_ref, noise_ref, probes_ref, weights_ref, load_sem,
+    col_pts, row_pts, vec, row_vec, part_out, part, dot_buf, k_hi, k_lo, right_fac, sq_dist,
+    pts_z_send, pts_z_recv, pts_q_send, pts_q_recv, vec_send, vec_recv, row_send, row_recv,
+    part_send, part_recv, dot_send, dot_recv,
 ):
-    n, m = probes_ref.shape
+    m, n = probes_ref.shape
     nq = ny * ns
     block = lax.axis_index("pts")
     core = lax.axis_index("sub")
@@ -85,9 +86,20 @@
     for i in range(1, nz * nq):
         pl.semaphore_signal(barrier, inc=1, device_id=device(*offsets[i]), device_id_type=MESH)
 
-    scaled = (points_ref[...] * (inverse_ref[...] * SQRT_FIVE)).T
+    loads = [
+        pltpu.make_async_copy(src, dst, load_sem.at[i])
+        for i, (src, dst) in enumerate((
+            (points_any, points_ref), (inverse_any, inverse_ref), (probes_any, probes_ref),
+            (noise_any, noise_ref), (weights_any, weights_ref),
+        ))
+    ]
+    for load in loads:
+        load.start()
+    for load in loads:
+        load.wait()
+    scaled = points_ref[...] * (inverse_ref[...] * SQRT_FIVE).T
     col_pts[0] = scaled
-    own_probes = probes_ref[...].T
+    own_probes = probes_ref[...]
     vec[0, 0] = own_probes
 
     pl.semaphore_wait(barrier, nz * nq - 1)
@@ -103,11 +115,20 @@
         for dz in range(1, nz):
             k = nz - dz
             send(vec.at[t, 0], vec.at[t, k], vec_send.at[t, k], vec_recv.at[t, k], device(dz, 0, 0))
+        for j in range(1, nq):
+            k = mirror_q(j)
+            send(vec.at[t, 0], row_vec.at[t, k], row_send.at[t, k], row_recv.at[t, k], device(0, *q_offsets[j]))
 
     def vector_block(t, k):
         if k:
             arrived(vec.at[t, k], vec_send.at[t, k], vec_recv.at[t, k])
         return vec[t, k]
+
+    def row_block(t, j):
+        if not j:
+            return vec[t, 0]
+        arrived(row_vec.at[t, j], row_send.at[t, j], row_recv.at[t, j])
+        return row_vec[t, j]
 
     gather_vector(0)
 
@@ -142,25 +163,27 @@
 
         lax.fori_loop(0, n // 16, rows, 0)
 
-    eye = lax.broadcasted_iota(jnp.int32, (m, 128), 0) == lax.broadcasted_iota(jnp.int32, (m, 128), 1)
-
-    def to_row(column):
-        return jnp.sum(jnp.where(eye, column, 0.0), axis=0, keepdims=True)
-
-    def to_column(row):
-        return jnp.sum(jnp.where(eye, row, 0.0), axis=1, keepdims=True)
+    line = lax.broadcasted_iota(jnp.int32, (m, 128), 0)
+    lane = lax.broadcasted_iota(jnp.int32, (m, 128), 1)
+
+    def to_row(columns):
+        return sum(
+            jnp.sum(jnp.where(lane == line + i * m, column, 0.0), axis=0, keepdims=True)
+            for i, column in enumerate(columns)
+        )
+
+    def to_column(row, i):
+        return jnp.sum(jnp.where(lane == line + i * m, row, 0.0), axis=1, keepdims=True)
+
+    def total(x):
+        return jnp.sum(x, axis=1, keepdims=True)
 
     noise = noise_ref[...]
-    residual = [vector_block(0, k) for k in range(nz)]
-    direction = image = norm_now = None
+    direction = image = norm_now = curve = None
     answer = jnp.zeros_like(own_probes)
     for t in range(ITERS):
-        norm_part = sum(jnp.sum(r * r, axis=1, keepdims=True) for r in residual)
-        rr_buf[t, 0] = to_row(norm_part)
-        for j in range(1, nq):
-            s = mirror_q(j)
-            send(rr_buf.at[t, 0], rr_buf.at[t, s], rr_send.at[t, s], rr_recv.at[t, s], device(0, *q_offsets[j]))
-        pieces = [halves(r) for r in residual]
+        own = vec[t, 0]
+        pieces = [halves(vector_block(t, k)) for k in range(nz)]
         hi = jnp.concatenate([p[0] for p in pieces], axis=1)
         lo = jnp.concatenate([p[1] for p in pieces], axis=1)
         both = jnp.concatenate([hi, lo], axis=0)
@@ -170,47 +193,44 @@
             two = jnp.dot(both, k_hi[:, span], preferred_element_type=F32)
             return two[:m] + two[m:] + jnp.dot(hi, k_lo[:, span], preferred_element_type=F32)
 
+        products = jnp.zeros_like(own)
         for j in reversed(range(1, nq)):
-            part_out[t, j] = partial(j)
+            term = partial(j)
+            part_out[t, j] = term
             s = mirror_q(j)
             send(part_out.at[t, j], part.at[t, s], part_send.at[t, s], part_recv.at[t, s], device(0, *q_offsets[j]))
-        fresh = partial(0) + noise * residual[0]
-        norm_row = rr_buf[t, 0]
-        for j in range(1, nq):
-            arrived(rr_buf.at[t, j], rr_send.at[t, j], rr_recv.at[t, j])
-            norm_row = norm_row + rr_buf[t, j]
-        norm_next = to_column(norm_row)
+            products = products + term * row_block(t, j)
+        fresh = partial(0) + noise * own
+        products = products + fresh * own
+        crossed = own * image if t else jnp.zeros_like(own)
+        dot_buf[t, 0] = to_row([total(products), total(own * own), total(crossed)])
+        for i in reversed(range(1, nz * nq)):
+            s = mirror(i)
+            send(dot_buf.at[t, 0], dot_buf.at[t, s], dot_send.at[t, s], dot_recv.at[t, s], device(*offsets[i]))
         for j in range(1, nq):
             arrived(part.at[t, j], part_send.at[t, j], part_recv.at[t, j])
             fresh = fresh + part[t, j]
+        sums = dot_buf[t, 0]
+        for i in range(1, nz * nq):
+            arrived(dot_buf.at[t, i], dot_send.at[t, i], dot_recv.at[t, i])
+            sums = sums + dot_buf[t, i]
+        norm_next = to_column(sums, 1)
         if t == 0:
-            image, direction = fresh, residual
+            image, direction, curve = fresh, own, to_column(sums, 0)
         else:
             beta = norm_next / norm_now
             image = fresh + beta * image
-            direction = [r + beta * d for r, d in zip(residual, direction)]
+            direction = own + beta * direction
+            curve = to_column(sums, 0) + beta * (2.0 * to_column(sums, 2) + beta * curve)
         norm_now = norm_next
+        alpha = norm_now / curve
+        residual = own - alpha * image
         if t + 1 < ITERS:
-            vec[t + 1, 0] = image
+            vec[t + 1, 0] = residual
             gather_vector(t + 1)
-        dot_buf[t, 0] = to_row(jnp.sum(direction[0] * image, axis=1, keepdims=True))
-        for i in range(1, nz * nq):
-            s = mirror(i)
-            send(dot_buf.at[t, 0], dot_buf.at[t, s], dot_send.at[t, s], dot_recv.at[t, s], device(*offsets[i]))
-        dot_row = dot_buf[t, 0]
-        for i in range(1, nz * nq):
-            arrived(dot_buf.at[t, i], dot_send.at[t, i], dot_recv.at[t, i])
-            dot_row = dot_row + dot_buf[t, i]
-        alpha = norm_now / to_column(dot_row)
-        answer = answer + alpha * direction[0]
-        if t + 1 < ITERS:
-            residual = [residual[0] - alpha * image] + [
-                residual[k] - alpha * vector_block(t + 1, k) for k in range(1, nz)
-            ]
-        else:
-            residual = [residual[0] - alpha * image]
-    sol_ref[...] = answer.T
-    res_ref[...] = residual[0].T
+        answer = answer + alpha * direction
+    sol_ref[...] = answer
+    res_ref[...] = residual
     for copy in sends:
         copy.wait_send()
 
@@ -226,19 +246,25 @@
         depth = 3 * features + (-3 * features) % 128
         vmem = pl.BlockSpec(memory_space=pltpu.VMEM)
         dma = pltpu.SemaphoreType.DMA
-        out = jax.ShapeDtypeStruct((n, m), F32)
-        return pl.pallas_call(
+        out = jax.ShapeDtypeStruct((m, n), F32)
+        answer, residual = pl.pallas_call(
             functools.partial(kernel, nz, ny, ns),
             out_shape=(out, out),
-            in_specs=[vmem] * 4 + [pl.BlockSpec(memory_space=pltpu.SMEM)],
+            in_specs=[pl.BlockSpec(memory_space=pltpu.HBM)] * 5,
             out_specs=(vmem, vmem),
             scratch_shapes=[
+                pltpu.VMEM((features, n), F32),
+                pltpu.VMEM((1, features), F32),
+                pltpu.VMEM((1, n), F32),
+                pltpu.VMEM((m, n), F32),
+                pltpu.SMEM(task_cov.shape, F32),
+                dma((5,)),
                 pltpu.VMEM((nz, features, n), F32),
                 pltpu.VMEM((nq, features, n), F32),
                 pltpu.VMEM((ITERS, nz, m, n), F32),
                 pltpu.VMEM((ITERS, nq, m, n), F32),
                 pltpu.VMEM((ITERS, nq, m, n), F32),
-                pltpu.VMEM((ITERS, nq, 1, 128), F32),
+                pltpu.VMEM((ITERS, nq, m, n), F32),
                 pltpu.VMEM((ITERS, nz * nq, 1, 128), F32),
                 pltpu.VMEM((nz * n, nq * n), BF16),
                 pltpu.VMEM((nz * n, nq * n), BF16),
@@ -251,9 +277,10 @@
                 dma((ITERS, nz * nq)), dma((ITERS, nz * nq)),
             ],
             compiler_params=pltpu.CompilerParams(
-                collective_id=0, has_side_effects=True, vmem_limit_bytes=48 * 2**20
+                collective_id=0, has_side_effects=True, vmem_limit_bytes=64 * 2**20
             ),
-        )(points, inverse_scale[None, :], noise_level[None, :], probes, task_cov)
+        )(points.T, inverse_scale[None, :], noise_level[None, :], probes.T, task_cov)
+        return answer.T, residual.T
 
     rows = P(("groups", "pts", "sub"), None)
     return jax.shard_map(

time: 50.1 us -> 49.2 us (0.982)
  local copies, waits for them, and re-layouts: 3 us -> 2 us
    pallas_call x2 -> x0, local copies, waits for them, and re-layouts: 1.38 us -> none  [local(): pl.pallas_call(functools.partial(kernel, nz, ny, ns), out_shape=(out, out...]
    unnamed x10 -> x4, local copies, waits for them, and re-layouts: 1.62 us -> 2 us
where the time goes in v2:
time: 49.2 us; the launch traced here: 49 us
  Pallas kernels  46.3 us (94%)
  local copies, waits for them, and re-layouts  2 us (4%)
  between operations  0.65 us (1%)
    pallas_call x1, Pallas kernels, local(): pl.pallas_call(functools.partial(kernel, nz, ny, ns), out_shape=(out, out...  46.3 us
    unnamed x4, local copies, waits for them, and re-layouts  2 us

profile of v2, /device:TPU:0, one launch (start us, length us, event | category | flops | bytes accessed | tf_op | source)
XLA Modules:
  0.0 49.0 jit_solution(2693522094841357018)
XLA Ops:
  0.6 46.3 %shard_map.68 = (f32[32,256]{1,0:T(8,128)}, f32[32,256]{1,0:T(8,128)}) custom-call(f32[64,256]{1,0:T(8,128)} %bitcast.6, f32[1,64]{1,0:T(1,128)} %bitcast.11, f32[1,256]{1,0:T(1,128)} %bitcast.10, f32[32,256]{1,0:T(8,128)} %bitcast.7, f32[8,8]{1,0:T(8,128)} %weights_any.1), custom_call_target="tpu_custom_call" | custom-call | tf_op jit(solution)/shard_map/pallas_call | solution.py:250
  47.0 0.0 copy-start
  47.0 1.4 %copy.9 = f32[256,32]{0,1:T(8,128)} copy(f32[256,32]{0,1:T(8,128)} %bitcast.9) | data formatting | bytes 65536
  48.4 0.0 copy-done
  48.4 0.6 %copy.10 = f32[256,32]{0,1:T(8,128)} copy(f32[256,32]{0,1:T(8,128)S(1)} %bitcast.8) | data formatting | bytes 65536
Async XLA Ops:
  47.0 1.4 %copy-start = (f32[32,256]{1,0:T(8,128)S(1)}, f32[32,256]{1,0:T(8,128)}, u32[]{:S(2)}) copy-start(f32[32,256]{1,0:T(8,128)} %get-tuple-element.5) | copy-start | bytes 98308

commit v3 on v2

--- a/solution.py
+++ b/solution.py
@@ -42,9 +42,9 @@
 def kernel(
     nz, ny, ns, points_any, inverse_any, noise_any, probes_any, weights_any, sol_ref, res_ref,
     points_ref, inverse_ref, noise_ref, probes_ref, weights_ref, load_sem,
-    col_pts, row_pts, vec, row_vec, part_out, part, dot_buf, k_hi, k_lo, right_fac, sq_dist,
+    col_pts, row_pts, vec, row_vec, part_out, part, rr_buf, dot_buf, k_hi, k_lo, right_fac, sq_dist,
     pts_z_send, pts_z_recv, pts_q_send, pts_q_recv, vec_send, vec_recv, row_send, row_recv,
-    part_send, part_recv, dot_send, dot_recv,
+    part_send, part_recv, rr_send, rr_recv, dot_send, dot_recv,
 ):
     m, n = probes_ref.shape
     nq = ny * ns
@@ -180,10 +180,31 @@
 
     noise = noise_ref[...]
     direction = image = norm_now = curve = None
+    steps = []
+    residual = [vector_block(0, k) for k in range(nz)]
     answer = jnp.zeros_like(own_probes)
+
+    def send_dots(t):
+        for i in reversed(range(1, nz * nq)):
+            s = mirror(i)
+            send(dot_buf.at[t, 0], dot_buf.at[t, s], dot_send.at[t, s], dot_recv.at[t, s], device(*offsets[i]))
+
+    def sum_dots(t):
+        sums = dot_buf[t, 0]
+        for i in range(1, nz * nq):
+            arrived(dot_buf.at[t, i], dot_send.at[t, i], dot_recv.at[t, i])
+            sums = sums + dot_buf[t, i]
+        return sums
+
     for t in range(ITERS):
-        own = vec[t, 0]
-        pieces = [halves(vector_block(t, k)) for k in range(nz)]
+        last = t + 1 == ITERS
+        own = residual[0]
+        if not last:
+            rr_buf[t, 0] = to_row([sum(total(r * r) for r in residual)])
+            for j in range(1, nq):
+                s = mirror_q(j)
+                send(rr_buf.at[t, 0], rr_buf.at[t, s], rr_send.at[t, s], rr_recv.at[t, s], device(0, *q_offsets[j]))
+        pieces = [halves(r) for r in residual]
         hi = jnp.concatenate([p[0] for p in pieces], axis=1)
         lo = jnp.concatenate([p[1] for p in pieces], axis=1)
         both = jnp.concatenate([hi, lo], axis=0)
@@ -199,38 +220,53 @@
             part_out[t, j] = term
             s = mirror_q(j)
             send(part_out.at[t, j], part.at[t, s], part_send.at[t, s], part_recv.at[t, s], device(0, *q_offsets[j]))
-            products = products + term * row_block(t, j)
+            if last:
+                row = row_block(0, j)
+                for i, step in enumerate(steps):
+                    row = row - step * row_block(i + 1, j)
+                products = products + term * row
         fresh = partial(0) + noise * own
-        products = products + fresh * own
-        crossed = own * image if t else jnp.zeros_like(own)
-        dot_buf[t, 0] = to_row([total(products), total(own * own), total(crossed)])
-        for i in reversed(range(1, nz * nq)):
-            s = mirror(i)
-            send(dot_buf.at[t, 0], dot_buf.at[t, s], dot_send.at[t, s], dot_recv.at[t, s], device(*offsets[i]))
+        if last:
+            products = products + fresh * own
+            crossed = own * image if t else jnp.zeros_like(own)
+            dot_buf[t, 0] = to_row([total(products), total(own * own), total(crossed)])
+            send_dots(t)
+        else:
+            norm_row = rr_buf[t, 0]
+            for j in range(1, nq):
+                arrived(rr_buf.at[t, j], rr_send.at[t, j], rr_recv.at[t, j])
+                norm_row = norm_row + rr_buf[t, j]
+            norm_next = to_column(norm_row, 0)
         for j in range(1, nq):
             arrived(part.at[t, j], part_send.at[t, j], part_recv.at[t, j])
             fresh = fresh + part[t, j]
-        sums = dot_buf[t, 0]
-        for i in range(1, nz * nq):
-            arrived(dot_buf.at[t, i], dot_send.at[t, i], dot_recv.at[t, i])
-            sums = sums + dot_buf[t, i]
-        norm_next = to_column(sums, 1)
+        if last:
+            sums = sum_dots(t)
+            norm_next = to_column(sums, 1)
         if t == 0:
-            image, direction, curve = fresh, own, to_column(sums, 0)
+            image, direction = fresh, own
         else:
             beta = norm_next / norm_now
             image = fresh + beta * image
             direction = own + beta * direction
-            curve = to_column(sums, 0) + beta * (2.0 * to_column(sums, 2) + beta * curve)
+        if last:
+            bent = to_column(sums, 0)
+            curve = bent + beta * (2.0 * to_column(sums, 2) + beta * curve) if t else bent
+        else:
+            dot_buf[t, 0] = to_row([total(direction * image)])
+            send_dots(t)
+            vec[t + 1, 0] = image
+            gather_vector(t + 1)
+            curve = to_column(sum_dots(t), 0)
         norm_now = norm_next
         alpha = norm_now / curve
-        residual = own - alpha * image
-        if t + 1 < ITERS:
-            vec[t + 1, 0] = residual
-            gather_vector(t + 1)
+        steps.append(alpha)
         answer = answer + alpha * direction
+        residual = [own - alpha * image] + [
+            residual[k] - alpha * vector_block(t + 1, k) for k in range(1, 1 if last else nz)
+        ]
     sol_ref[...] = answer
-    res_ref[...] = residual
+    res_ref[...] = residual[0]
     for copy in sends:
         copy.wait_send()
 
@@ -265,6 +301,7 @@
                 pltpu.VMEM((ITERS, nq, m, n), F32),
                 pltpu.VMEM((ITERS, nq, m, n), F32),
                 pltpu.VMEM((ITERS, nq, m, n), F32),
+                pltpu.VMEM((ITERS, nq, 1, 128), F32),
                 pltpu.VMEM((ITERS, nz * nq, 1, 128), F32),
                 pltpu.VMEM((nz * n, nq * n), BF16),
                 pltpu.VMEM((nz * n, nq * n), BF16),
@@ -274,6 +311,7 @@
                 dma((ITERS, nz)), dma((ITERS, nz)),
                 dma((ITERS, nq)), dma((ITERS, nq)),
                 dma((ITERS, nq)), dma((ITERS, nq)),
+                dma((ITERS, nq)), dma((ITERS, nq)),
                 dma((ITERS, nz * nq)), dma((ITERS, nz * nq)),
             ],
             compiler_params=pltpu.CompilerParams(

time: 49.2 us -> 45.7 us (0.929)
  Pallas kernels: 46.3 us -> 42.8 us
    pallas_call x1, Pallas kernels: 46.3 us -> 42.8 us  [local(): pl.pallas_call(functools.partial(kernel, nz, ny, ns), out_shape=(out, out...]
where the time goes in v3:
time: 45.7 us; the launch traced here: 45.5 us
  Pallas kernels  42.8 us (94%)
  local copies, waits for them, and re-layouts  2 us (4%)
  between operations  0.65 us (1%)
    pallas_call x1, Pallas kernels, local(): pl.pallas_call(functools.partial(kernel, nz, ny, ns), out_shape=(out, out...  42.8 us
    unnamed x4, local copies, waits for them, and re-layouts  2 us

profile of v3, /device:TPU:0, one launch (start us, length us, event | category | flops | bytes accessed | tf_op | source)
XLA Modules:
  0.0 45.5 jit_solution(518144919581479044)
XLA Ops:
  0.6 42.8 %shard_map.68 = (f32[32,256]{1,0:T(8,128)}, f32[32,256]{1,0:T(8,128)}) custom-call(f32[64,256]{1,0:T(8,128)} %bitcast.6, f32[1,64]{1,0:T(1,128)} %bitcast.11, f32[1,256]{1,0:T(1,128)} %bitcast.10, f32[32,256]{1,0:T(8,128)} %bitcast.7, f32[8,8]{1,0:T(8,128)} %weights_any.1), custom_call_target="tpu_custom_call" | custom-call | tf_op jit(solution)/shard_map/pallas_call | solution.py:286
  43.5 0.0 copy-start
  43.5 1.4 %copy.9 = f32[256,32]{0,1:T(8,128)} copy(f32[256,32]{0,1:T(8,128)} %bitcast.9) | data formatting | bytes 65536
  44.8 0.0 copy-done
  44.8 0.6 %copy.10 = f32[256,32]{0,1:T(8,128)} copy(f32[256,32]{0,1:T(8,128)S(1)} %bitcast.8) | data formatting | bytes 65536
Async XLA Ops:
  43.5 1.4 %copy-start = (f32[32,256]{1,0:T(8,128)S(1)}, f32[32,256]{1,0:T(8,128)}, u32[]{:S(2)}) copy-start(f32[32,256]{1,0:T(8,128)} %get-tuple-element.5) | copy-start | bytes 98308

commit v4 on v3

--- a/solution.py
+++ b/solution.py
@@ -161,7 +161,7 @@
                 k_lo[pl.ds(k * n + at, 16), span] = lo
             return carry
 
-        lax.fori_loop(0, n // 16, rows, 0)
+        lax.fori_loop(0, n // 16, rows, 0, unroll=4)
 
     line = lax.broadcasted_iota(jnp.int32, (m, 128), 0)
     lane = lax.broadcasted_iota(jnp.int32, (m, 128), 1)

time: 45.7 us -> 45.4 us (level)
  no operation moved by 1% of the time
where the time goes in v4:
time: 45.4 us; the launch traced here: 45.2 us
  Pallas kernels  42.6 us (94%)
  local copies, waits for them, and re-layouts  2 us (4%)
  between operations  0.65 us (1%)
    pallas_call x1, Pallas kernels, local(): pl.pallas_call(functools.partial(kernel, nz, ny, ns), out_shape=(out, out...  42.6 us
    unnamed x4, local copies, waits for them, and re-layouts  2 us

profile of v4, /device:TPU:0, one launch (start us, length us, event | category | flops | bytes accessed | tf_op | source)
XLA Modules:
  0.0 45.2 jit_solution(3850384144504303504)
XLA Ops:
  0.6 42.6 %shard_map.68 = (f32[32,256]{1,0:T(8,128)}, f32[32,256]{1,0:T(8,128)}) custom-call(f32[64,256]{1,0:T(8,128)} %bitcast.6, f32[1,64]{1,0:T(1,128)} %bitcast.11, f32[1,256]{1,0:T(1,128)} %bitcast.10, f32[32,256]{1,0:T(8,128)} %bitcast.7, f32[8,8]{1,0:T(8,128)} %weights_any.1), custom_call_target="tpu_custom_call" | custom-call | tf_op jit(solution)/shard_map/pallas_call | solution.py:286
  43.2 0.0 copy-start
  43.2 1.4 %copy.9 = f32[256,32]{0,1:T(8,128)} copy(f32[256,32]{0,1:T(8,128)} %bitcast.9) | data formatting | bytes 65536
  44.6 0.0 copy-done
  44.6 0.6 %copy.10 = f32[256,32]{0,1:T(8,128)} copy(f32[256,32]{0,1:T(8,128)S(1)} %bitcast.8) | data formatting | bytes 65536
Async XLA Ops:
  43.2 1.4 %copy-start = (f32[32,256]{1,0:T(8,128)S(1)}, f32[32,256]{1,0:T(8,128)}, u32[]{:S(2)}) copy-start(f32[32,256]{1,0:T(8,128)} %get-tuple-element.5) | copy-start | bytes 98308
